TPU v7x, 32 devices: a whole 2x2x4 slice. The times are simulated.
32 devices in a mesh: cells: 8 (over z, x), snap: 4 (over y, core).
Axes of the slice: x: 2, y: 2, z: 4, core: 2. Of those that a mesh axis runs over, the one named last changes fastest.
Arguments:
- temporal_modes: bfloat16 [256, 4096], P('cells', 'snap'), may hold values from -0.09375 to 0.09375
- volume_field: bfloat16 [4096, 20480], P('snap', 'cells'), may hold values from -6 to 6
- mass_root: float32 [20480], P('cells'), may hold values from 0.3 to 3
- wall_pressure: bfloat16 [5120, 4096], P('cells', 'snap'), may hold values from -6 to 6
- face_area: bfloat16 [5120], P('cells'), may hold values from 0.099609375 to 10
- face_count: int32 [8], P('cells'), may hold values from 0 to 640, as said below
Outputs:
- extended_modes: bfloat16 [256, 20480], P('snap', 'cells')
- wall_modes: bfloat16 [5120, 256], P('cells')
Inputs may be any that keep to these rules, and one draw needn't show every extreme that they name: `face_count`: exactly 2 partitions have live wall faces, each between 320 and 640 of them, and one has exactly 640; every other partition has none.
All inputs are finite; a program needn't handle non-finite values.
Results may differ from a plain program's by a relative error of at most 0.013.
Values may be sent and summed in bfloat16 or wider, within the bound.
A program may use at most 64 MiB of HBM per device.

v0:
```python
import jax
import jax.numpy as jnp
from jax import lax
from jax.sharding import PartitionSpec as P


def contract(rows_data, modes_full):
    return lax.dot_general(
        rows_data, modes_full, (((1,), (1,)), ((), ())), preferred_element_type=jnp.float32
    )


def body(temporal_modes, volume_field, mass_root, wall_pressure, face_area, face_count):
    modes_full = lax.all_gather(temporal_modes, "cells", axis=0, tiled=True)
    face_slots = wall_pressure.shape[0]
    mode_count = modes_full.shape[0]
    live_flat = jnp.arange(face_slots, dtype=jnp.int32) < face_count[0]
    weights = jnp.where(live_flat, face_area.astype(jnp.float32), jnp.float32(0.0))
    wall_coef = lax.psum(contract(wall_pressure, modes_full).astype(jnp.bfloat16), "snap").astype(
        jnp.float32
    )
    energy_part = jnp.sum(weights[:, None] * wall_coef * wall_coef, axis=0)
    area_part = jnp.sum(weights)
    energy, area_total = lax.psum((energy_part, area_part), "cells")
    inverse = lax.rsqrt(energy / area_total + 1e-06)
    normed = jnp.where(live_flat[:, None], wall_coef * inverse[None, :], jnp.float32(0.0))
    wall_modes = normed.astype(jnp.bfloat16)
    my_rows = mode_count // lax.axis_size("snap")
    summed = lax.psum_scatter(
        jnp.dot(modes_full, volume_field, preferred_element_type=jnp.float32).astype(jnp.bfloat16),
        "snap",
        scatter_dimension=0,
        tiled=True,
    ).astype(jnp.float32)
    my_inverse = lax.dynamic_slice_in_dim(inverse, lax.axis_index("snap") * my_rows, my_rows, 0)
    scaled = summed * mass_root[None, :] * my_inverse[:, None]
    return (scaled.astype(jnp.bfloat16), wall_modes)


def solution(mesh):
    in_specs = (
        P("cells", "snap"),
        P("snap", "cells"),
        P("cells"),
        P("cells", "snap"),
        P("cells"),
        P("cells"),
    )
    out_specs = (P("snap", "cells"), P("cells", None))
    return jax.shard_map(body, mesh=mesh, in_specs=in_specs, out_specs=out_specs, check_vma=False)
```

profile of v0, /device:TPU:0, one launch (start us, length us, event | category | flops | bytes accessed | tf_op | source)
XLA Modules:
  0.0 113.3 jit_solution(16698330735532449738)
XLA Ops:
  7.2 0.0 copy-start
  7.2 0.0 all-reduce.3.cloned.1.call-start
  7.2 33.4 %all_gather.3 = bf16[256,1024]{1,0:T(8,128)(2,1)S(1)} all-gather(bf16[32,1024]{1,0:T(8,128)(2,1)} %param.6), channel_id=1, replica_groups=mesh['cells'=8,'snap'=4] {'cells'}, dimensions={0}, use_global_device_ids=true | all-gather | bytes 589824 | tf_op jit(solution)/shard_map/all_gather | solution.py:14
  40.6 0.0 copy-done
  40.6 1.3 %convolution_convert_fusion.1 = bf16[640,256]{1,0:T(8,128)(2,1)} fusion(bf16[640,1024]{1,0:T(8,128)(2,1)S(1)} %copy-done, bf16[256,1024]{1,0:T(8,128)(2,1)S(1)} %all_gather.3), kind=kOutput, calls=%fused_computation.1 | convolution fusion | flops 335708160 | bytes 2162688 | tf_op jit(solution)/shard_map/dot_general | solution.py:8
  41.9 0.0 all-reduce.3.cloned.1.call-update
  41.9 0.0 reduce-scatter.2.cloned.1.call-start
  41.9 5.1 %convolution_convert_fusion = bf16[256,2560]{1,0:T(8,128)(2,1)} fusion(bf16[256,1024]{1,0:T(8,128)(2,1)S(1)} %all_gather.3, bf16[1024,2560]{1,0:T(8,128)(2,1)} %param.7), kind=kOutput, calls=%fused_computation | convolution fusion | flops 1342832640 | bytes 7077888 | tf_op jit(solution)/shard_map/dot_general | solution.py:30
  47.0 0.0 copy-start.2
  47.0 0.0 copy-start.1
  47.0 0.0 reduce-scatter.2.cloned.1.call-update
  47.7 0.0 copy-done.2
  47.7 0.6 fusion.3
  48.4 27.1 %all-reduce.3.cloned.1.call-done = bf16[640,256]{1,0:T(8,128)(2,1)} async-done(((bf16[640,256]{1,0:T(8,128)(2,1)}), bf16[640,256]{1,0:T(8,128)(2,1)}) %all-reduce.3.cloned.1.call-update) | async-done | bytes 327696 | tf_op jit(solution)/shard_map/psum | solution.py:19
  75.5 1.1 %fusion.2 = f32[256]{0:T(256)S(1)} fusion(bf16[640,256]{1,0:T(8,128)(2,1)} %all-reduce.3.cloned.1.call-done, f32[640]{0:T(1024)S(1)} %get-tuple-element.5), kind=kLoop, calls=%fused_computation.6 | loop fusion | flops 655104 | bytes 331264 | tf_op jit(solution)/shard_map/reduce_sum | solution.py:22
  76.6 21.9 %all-reduce = (f32[256]{0:T(256)S(1)}, f32[]{:T(128)}) all-reduce(f32[256]{0:T(256)S(1)} %fusion.2, f32[]{:T(128)} %get-tuple-element.4), channel_id=1, replica_groups=mesh['cells'=8,'snap'=4] {'cells'}, use_global_device_ids=true, to_apply=%region_3.4 | all-reduce | flops 257 | bytes 2056 | tf_op jit(solution)/shard_map/psum | solution.py:24
  98.5 0.7 add_rsqrt_fusion
  99.2 0.1 dynamic_slice.3
  99.2 1.9 %fusion.1 = bf16[640,256]{1,0:T(8,128)(2,1)} fusion(bf16[640,256]{1,0:T(8,128)(2,1)} %all-reduce.3.cloned.1.call-done, f32[256]{0:T(256)S(1)} %add_rsqrt_fusion, pred[640]{0:T(1024)(128)(4,1)S(1)} %iota_compare_fusion), kind=kLoop, calls=%fused_computation.5 | loop fusion | flops 655360 | bytes 657024 | tf_op jit(solution)/shard_map/convert_element_type | solution.py:27
  101.1 3.5 %reduce-scatter.2.cloned.1.call-done = bf16[64,2560]{1,0:T(8,128)(2,1)} async-done(((bf16[256,2560]{1,0:T(8,128)(2,1)}), bf16[64,2560]{1,0:T(8,128)(2,1)}) %reduce-scatter.2.cloned.1.call-update) | async-done | bytes 327696 | tf_op jit(solution)/shard_map/reduce_scatter | solution.py:29
  104.6 0.0 copy-done.1
  104.6 1.8 %multiply_convert_fusion = bf16[64,2560]{1,0:T(8,128)(2,1)} fusion(bf16[64,2560]{1,0:T(8,128)(2,1)} %reduce-scatter.2.cloned.1.call-done, f32[64]{0:T(128)S(1)} %dynamic_slice.3, f32[2560]{0:T(1024)S(1)} %copy-done.1), kind=kLoop, calls=%fused_computation.7 | loop fusion | flops 655360 | bytes 665856 | tf_op jit(solution)/shard_map/convert_element_type | solution.py:37
  (1 shorter events, 0.0 us)
Async XLA Ops:
  7.2 33.4 %copy-start = (bf16[640,1024]{1,0:T(8,128)(2,1)S(1)}, bf16[640,1024]{1,0:T(8,128)(2,1)}, u32[]{:S(2)}) copy-start(bf16[640,1024]{1,0:T(8,128)(2,1)} %param.9) | copy-start | bytes 3932164
  7.2 68.3 %all-reduce.3.cloned.1.call-start = ((), (), s32[]{:S(2)}) async-start(), calls=%async_computation.2 | async-start | bytes 655360 | tf_op jit(solution)/shard_map/psum | solution.py:19
  41.9 62.7 %reduce-scatter.2.cloned.1.call-start = ((), (), s32[]{:S(2)}) async-start(), calls=%async_computation.1 | async-start | bytes 1638400 | tf_op jit(solution)/shard_map/reduce_scatter | solution.py:29
  47.0 0.7 copy-start.2
  47.0 57.6 %copy-start.1 = (f32[2560]{0:T(1024)S(1)}, f32[2560]{0:T(1024)}, u32[]{:S(2)}) copy-start(f32[2560]{0:T(1024)} %param.8) | copy-start | bytes 30724
Sparse Core Ops, SparseCore 0:
  42.0 33.4 all-reduce.2
  78.0 26.5 reduce-scatter.1
where the time goes:
time: 114 us; the launch traced here: 113 us
  blocking collectives  55.2 us (48%)
  waiting for transfers between devices  30.7 us (27%)
  between operations  14.7 us (13%)
  matrix products  6.37 us (6%)
  other arithmetic  6.07 us (5%)
    all_gather x1, blocking collectives, body(): modes_full = lax.all_gather(temporal_modes, 'cells', axis=0, tiled=True)  33.4 us
    psum x1, waiting for transfers between devices, body(): lax.psum(contract(wall_pressure, modes_full).astype(jnp.bfloat16), 'snap')  27.1 us
    psum x1, blocking collectives, body(): energy, area_total = lax.psum((energy_part, area_part), 'cells')  21.9 us
    dot_general x1, matrix products, body(): jnp.dot(modes_full, volume_field, preferred_element_type=jnp.float32)  5.09 us
    reduce_scatter x1, waiting for transfers between devices, body(): lax.psum_scatter(jnp.dot(modes_full, volume_field, preferred_element_type...  3.53 us
  transfers between devices with their start and end apart: 2, of which 2 were waited for; matrix products, arithmetic and copies ran while one was open for 8% of the time, Pallas kernels for 0%

commit v1 on v0

v1 whole, which is shorter than its diff:
```python
import functools

import jax
import jax.numpy as jnp
from jax import lax
from jax.experimental import pallas as pl
from jax.experimental.pallas import tpu as pltpu
from jax.sharding import PartitionSpec as P

MESH = pl.DeviceIdType.MESH
F32 = jnp.float32
BF16 = jnp.bfloat16
LANES = 128


def kernel(
    n, lines, pieces,
    modes_ref, vol_ref, mass_ref, press_ref, area_ref, count_ref,
    ext_ref, wall_ref,
    gbuf, perm, vbuf, pbuf, wcol,
    w_send, w_recv, w_keep, wy_send, wy_recv, coef,
    p_send, p_recv, p_keep, py_send, py_recv,
    e_send, e_recv, inv_row, inv_col, ext_buf, wall_buf,
    load_sem, g_send_sem, g_recv_sem, w_sem, p_sem, py_sem, e_send_sem, e_recv_sem, out_sem,
):
    cell, snap = lax.axis_index("cells"), lax.axis_index("snap")
    y, core = snap // 2, snap % 2
    group = n // lines
    z, x = cell // group, cell % group
    mate = (cell, y * 2 + 1 - core)
    across = (cell, (1 - y) * 2 + core)
    others = [(lax.rem(cell + d, n), snap) for d in range(1, n)]
    mode_count, depth = perm.shape
    share = mode_count // 4
    per_share = n // 4
    half = pbuf.shape[1]
    width = vbuf.shape[2]
    slots = 2 * half

    def remote(src, dst, send, recv, to):
        return pltpu.make_async_remote_copy(
            src_ref=src, dst_ref=dst, send_sem=send, recv_sem=recv,
            device_id=to, device_id_type=MESH,
        )

    own_copy = pltpu.make_async_copy(modes_ref, gbuf.at[cell], load_sem.at[0])
    own_copy.start()
    press_copies = [
        pltpu.make_async_copy(press_ref.at[pl.ds(h * half, half)], pbuf.at[h], load_sem.at[1 + h])
        for h in range(2)
    ]
    vol_copies = [
        pltpu.make_async_copy(vol_ref.at[:, pl.ds(j * width, width)], vbuf.at[j], load_sem.at[3 + j])
        for j in range(pieces)
    ]
    for copy in press_copies + vol_copies:
        copy.start()

    barrier = pltpu.get_barrier_semaphore()
    greeted = others + [mate, across]
    for other in greeted:
        pl.semaphore_signal(barrier, inc=1, device_id=other, device_id_type=MESH)
    pl.semaphore_wait(barrier, len(greeted))

    sent = []
    beside = [z * group + lax.rem(x + d, group) for d in range(1, group)]
    for d, to in enumerate(beside):
        copy = remote(modes_ref, gbuf.at[cell], g_send_sem.at[0, d], g_recv_sem.at[cell], (to, snap))
        copy.start()
        sent.append(copy)
    along = [lax.rem(z + d, lines) * group + x for d in range(1, lines)]
    for d, to in enumerate(along):
        copy = remote(
            modes_ref, gbuf.at[cell], g_send_sem.at[0, group - 1 + d], g_recv_sem.at[cell], (to, snap)
        )
        copy.start()
        sent.append(copy)

    slot_row = lax.broadcasted_iota(jnp.int32, (1, LANES), 1)
    count = count_ref[0]
    area_lanes = jnp.zeros((1, LANES), F32)
    for i in range(slots // LANES):
        row = area_ref[i : i + 1, :].astype(F32)
        row = jnp.where(slot_row + i * LANES < count, row, 0.0)
        area_lanes = area_lanes + row
        wcol[pl.ds(i * LANES, LANES), :] = jnp.broadcast_to(row, (LANES, LANES)).T

    for d, origin in enumerate(along):
        remote(
            gbuf.at[origin], gbuf.at[origin], g_send_sem.at[0, 0], g_recv_sem.at[origin], (origin, snap)
        ).wait_recv()
        for i, to in enumerate(beside):
            copy = remote(
                gbuf.at[origin], gbuf.at[origin], g_send_sem.at[1 + d, i], g_recv_sem.at[origin], (to, snap)
            )
            copy.start()
            sent.append(copy)
    own_copy.wait()
    for side in beside:
        for d in range(lines):
            origin = lax.rem(z + d, lines) * group + lax.rem(side, group)
            remote(
                gbuf.at[origin], gbuf.at[origin], g_send_sem.at[0, 0], g_recv_sem.at[origin], (side, snap)
            ).wait_recv()

    all_modes = gbuf[...].reshape(mode_count, depth).astype(BF16)
    for copy in press_copies:
        copy.wait()

    def contract(h):
        return lax.dot_general(
            pbuf[h], all_modes, (((1,), (1,)), ((), ())), preferred_element_type=F32
        )

    w_send[...] = contract(1 - core).astype(BF16)
    w_mate = remote(w_send, w_recv, w_sem.at[0], w_sem.at[1], mate)
    w_mate.start()
    w_keep[...] = contract(core)

    order = [
        (1 - y) * 2 + 1 - core, y * 2 + 1 - core, (1 - y) * 2 + core, y * 2 + core,
    ]
    for i, s in enumerate(order):
        perm[pl.ds(i * share, share), :] = (
            gbuf[pl.ds(s * per_share, per_share)].reshape(share, depth).astype(BF16)
        )

    p_copies, py_copies = [], []

    def project(j):
        vol_copies[j].wait()
        part = jnp.dot(perm[...], vbuf[j], preferred_element_type=F32)
        p_send[j] = part[: 2 * share].astype(BF16)
        copy = remote(p_send.at[j], p_recv.at[j], p_sem.at[0, j], p_sem.at[1, j], mate)
        copy.start()
        p_copies.append(copy)
        p_keep[j] = part[2 * share :]

    def pass_on(j):
        p_copies[j].wait_recv()
        both = p_keep[j] + p_recv[j].astype(F32)
        py_send[j] = both[:share].astype(BF16)
        copy = remote(py_send.at[j], py_recv.at[j], py_sem.at[0, j], py_sem.at[1, j], across)
        copy.start()
        py_copies.append(copy)
        p_keep[j, share:, :] = both[share:]

    project(0)
    w_mate.wait_recv()
    wy_send[...] = (w_keep[...] + w_recv[...].astype(F32)).astype(BF16)
    w_across = remote(wy_send, wy_recv, w_sem.at[2], w_sem.at[3], across)
    w_across.start()
    for j in range(1, pieces):
        project(j)
        pass_on(j - 1)
    pass_on(pieces - 1)

    w_across.wait_recv()
    coef[core] = (wy_send[...].astype(F32) + wy_recv[...].astype(F32)).astype(BF16)
    w_back = remote(coef.at[core], coef.at[core], w_sem.at[4], w_sem.at[5], mate)
    w_back.start()
    remote(coef.at[1 - core], coef.at[1 - core], w_sem.at[4], w_sem.at[5], mate).wait_recv()

    energy = jnp.zeros((1, mode_count), F32)
    for h in range(2):
        for lower in range(0, half, 64):
            value = coef[h, lower : lower + 64, :].astype(F32)
            weight = wcol[h * half + lower : h * half + lower + 64, 0:1]
            energy = energy + jnp.sum(weight * value * value, axis=0, keepdims=True)
    rows = mode_count // LANES
    e_send[...] = jnp.concatenate(
        [energy[:, i * LANES : (i + 1) * LANES] for i in range(rows)]
        + [area_lanes, jnp.zeros((8 - rows - 1, LANES), F32)],
        axis=0,
    )
    e_recv[cell] = e_send[...]
    e_copies = []
    for d, to in enumerate(others):
        copy = remote(e_send, e_recv.at[cell], e_send_sem.at[d], e_recv_sem.at[cell], to)
        copy.start()
        e_copies.append(copy)
    for other in others:
        origin = other[0]
        remote(
            e_send, e_recv.at[origin], e_send_sem.at[0], e_recv_sem.at[origin], other
        ).wait_recv()
    total = jnp.sum(e_recv[...], axis=0)
    area_total = jnp.sum(total[rows : rows + 1, :], axis=1, keepdims=True)
    inverse = lax.rsqrt(total[:rows, :] / area_total + 1e-06)
    inv_row[...] = inverse.reshape(rows, 1, LANES)

    flat = jnp.concatenate([inverse[i : i + 1, :] for i in range(rows)], axis=1)
    for h in range(2):
        for lower in range(0, half, 64):
            at = h * half + lower
            live = lax.broadcasted_iota(jnp.int32, (64, 1), 0) + at < count
            value = coef[h, lower : lower + 64, :].astype(F32) * flat
            wall_buf[at : at + 64, :] = jnp.where(live, value, 0.0).astype(BF16)
    wall_out = pltpu.make_async_copy(wall_buf, wall_ref, out_sem.at[0])
    wall_out.start()

    turned = jnp.broadcast_to(inv_row[y], (LANES, LANES)).T
    inv_col[...] = turned.reshape(2, share, LANES)
    mine = inv_col[core][:, 0:1]
    outs = [wall_out]
    for j in range(pieces):
        py_copies[j].wait_recv()
        summed = p_keep[j, share:, :] + py_recv[j].astype(F32)
        scaled = summed * mass_ref[:, j * width : (j + 1) * width] * mine
        ext_buf[j] = scaled.astype(BF16)
        copy = pltpu.make_async_copy(
            ext_buf.at[j], ext_ref.at[:, pl.ds(j * width, width)], out_sem.at[1 + j]
        )
        copy.start()
        outs.append(copy)

    for copy in sent + [w_mate, w_across, w_back] + p_copies + py_copies + e_copies:
        copy.wait_send()
    for copy in outs:
        copy.wait()


def body(n, temporal_modes, volume_field, mass_root, wall_pressure, face_area, face_count):
    rows, depth = temporal_modes.shape
    mode_count = rows * n
    cells = volume_field.shape[1]
    slots = wall_pressure.shape[0]
    half = slots // 2
    lines = 4
    pieces = 5
    width = cells // pieces
    share = mode_count // 4
    moved = BF16 if rows % 16 == 0 else F32
    group = n // lines
    dma = pltpu.SemaphoreType.DMA
    hbm, vmem, smem = (pl.BlockSpec(memory_space=m) for m in (pl.ANY, pltpu.VMEM, pltpu.SMEM))
    return pl.pallas_call(
        functools.partial(kernel, n, lines, pieces),
        out_shape=(
            jax.ShapeDtypeStruct((share, cells), BF16),
            jax.ShapeDtypeStruct((slots, mode_count), BF16),
        ),
        in_specs=[hbm, hbm, vmem, hbm, vmem, smem],
        out_specs=(hbm, hbm),
        scratch_shapes=[
            pltpu.VMEM((n, rows, depth), moved),
            pltpu.VMEM((mode_count, depth), BF16),
            pltpu.VMEM((pieces, depth, width), BF16),
            pltpu.VMEM((2, half, depth), BF16),
            pltpu.VMEM((slots, LANES), F32),
            pltpu.VMEM((half, mode_count), BF16),
            pltpu.VMEM((half, mode_count), BF16),
            pltpu.VMEM((half, mode_count), F32),
            pltpu.VMEM((half, mode_count), BF16),
            pltpu.VMEM((half, mode_count), BF16),
            pltpu.VMEM((2, half, mode_count), BF16),
            pltpu.VMEM((pieces, 2 * share, width), BF16),
            pltpu.VMEM((pieces, 2 * share, width), BF16),
            pltpu.VMEM((pieces, 2 * share, width), F32),
            pltpu.VMEM((pieces, share, width), BF16),
            pltpu.VMEM((pieces, share, width), BF16),
            pltpu.VMEM((8, LANES), F32),
            pltpu.VMEM((n, 8, LANES), F32),
            pltpu.VMEM((mode_count // LANES, 1, LANES), F32),
            pltpu.VMEM((2, share, LANES), F32),
            pltpu.VMEM((pieces, share, width), BF16),
            pltpu.VMEM((slots, mode_count), BF16),
            dma((3 + pieces,)),
            dma((lines, group - 1 + lines)),
            dma((n,)),
            dma((6,)),
            dma((2, pieces)),
            dma((2, pieces)),
            dma((n,)),
            dma((n,)),
            dma((1 + pieces,)),
        ],
        compiler_params=pltpu.CompilerParams(
            collective_id=0, has_side_effects=True, vmem_limit_bytes=40 * 1024 * 1024
        ),
    )(
        temporal_modes.astype(moved),
        volume_field,
        mass_root.reshape(1, cells),
        wall_pressure,
        face_area.reshape(slots // LANES, LANES),
        face_count,
    )


def solution(mesh):
    in_specs = (
        P("cells", "snap"),
        P("snap", "cells"),
        P("cells"),
        P("cells", "snap"),
        P("cells"),
        P("cells"),
    )
    out_specs = (P("snap", "cells"), P("cells", None))
    return jax.shard_map(
        functools.partial(body, mesh.shape["cells"]),
        mesh=mesh, in_specs=in_specs, out_specs=out_specs, check_vma=False,
    )
```

time: 114 us -> 41.9 us (0.37)
  blocking collectives: 55.2 us -> 0 us
  Pallas kernels: 0 us -> 32.8 us
  waiting for transfers between devices: 30.7 us -> 0 us
  between operations: 14.7 us -> 1.29 us
  local copies, waits for them, and re-layouts: 0.1 us -> 7.48 us
  matrix products: 6.37 us -> 0 us
  other arithmetic: 6.07 us -> 0 us
    all_gather x1 -> x0, blocking collectives: 33.4 us -> none  [body(): modes_full = lax.all_gather(temporal_modes, 'cells', axis=0, tiled=True)]
    pallas_call x0 -> x1, Pallas kernels: none -> 32.8 us  [body(): pl.pallas_call(functools.partial(kernel, n, lines, pieces), out_shape=(ja...]
    psum x1 -> x0, waiting for transfers between devices: 27.1 us -> none  [body(): lax.psum(contract(wall_pressure, modes_full).astype(jnp.bfloat16), 'snap')]
    psum x1 -> x0, blocking collectives: 21.9 us -> none  [body(): energy, area_total = lax.psum((energy_part, area_part), 'cells')]
    unnamed x6 -> x10, local copies, waits for them, and re-layouts: 0.02 us -> 6.77 us
    dot_general x2 -> x0, matrix products: 6.37 us -> none  [the longest x1 5.09 us: body(): jnp.dot(modes_full, volume_field, preferred_element_type=jnp.float32)]
    convert_element_type x2 -> x0, other arithmetic: 3.66 us -> none  [the longest x1 1.86 us: body(): wall_modes = normed.astype(jnp.bfloat16)]
    reduce_scatter x1 -> x0, waiting for transfers between devices: 3.53 us -> none  [body(): lax.psum_scatter(jnp.dot(modes_full, volume_field, preferred_element_type...]
  transfers between devices with their start and end apart: 2 -> 0, of which waited for: 2 -> 0; matrix products, arithmetic and copies ran while one was open for 8% -> 0% of each run, Pallas kernels for 0% -> 0%
where the time goes in v1:
time: 41.9 us; the launch traced here: 41.6 us
  Pallas kernels  32.8 us (78%)
  local copies, waits for them, and re-layouts  7.48 us (18%)
  between operations  1.29 us (3%)
    pallas_call x1, Pallas kernels, body(): pl.pallas_call(functools.partial(kernel, n, lines, pieces), out_shape=(ja...  32.8 us
    unnamed x10, local copies, waits for them, and re-layouts  6.77 us

profile of v1, /device:TPU:0, one launch (start us, length us, event | category | flops | bytes accessed | tf_op | source)
XLA Modules:
  0.0 41.6 jit_solution(8199702741341207512)
XLA Ops:
  1.3 0.7 %reshape.10.mass_ref = f32[1,2560]{1,0:T(1,128)S(1)} reshape(f32[2560]{0:T(1024)} %param.8) | data formatting | bytes 20480 | tf_op jit(solution)/shard_map/reshape | solution.py:284
  2.0 0.0 copy-start
  2.0 2.5 %copy-done = bf16[1024,2560]{1,0:T(8,128)(2,1)S(1)} copy-done((bf16[1024,2560]{1,0:T(8,128)(2,1)S(1)}, bf16[1024,2560]{1,0:T(8,128)(2,1)}, u32[]{:S(2)}) %copy-start) | copy-done | bytes 5242904
  4.5 0.0 copy-start.1
  4.5 1.3 %copy-done.1 = bf16[640,1024]{1,0:T(8,128)(2,1)S(1)} copy-done((bf16[640,1024]{1,0:T(8,128)(2,1)S(1)}, bf16[640,1024]{1,0:T(8,128)(2,1)}, u32[]{:S(2)}) %copy-start.1) | copy-done | bytes 1310744
  5.8 0.0 copy-start.2
  5.8 0.8 %copy-done.2 = bf16[32,1024]{1,0:T(8,128)(2,1)S(1)} copy-done((bf16[32,1024]{1,0:T(8,128)(2,1)S(1)}, bf16[32,1024]{1,0:T(8,128)(2,1)}, u32[]{:S(2)}) %copy-start.2) | copy-done | bytes 65560
  6.6 0.0 copy-start.3
  6.6 0.7 %copy-done.3 = bf16[640]{0:T(1024)(128)(2,1)S(1)} copy-done((bf16[640]{0:T(1024)(128)(2,1)S(1)}, bf16[640]{0:T(1024)(128)(2,1)}, u32[]{:S(2)}) %copy-start.3) | copy-done | bytes 1304
  7.3 32.8 %shard_map.77 = (bf16[64,2560]{1,0:T(8,128)(2,1)S(1)}, bf16[640,256]{1,0:T(8,128)(2,1)S(1)}) custom-call(bf16[32,1024]{1,0:T(8,128)(2,1)S(1)} %copy-done.2, bf16[1024,2560]{1,0:T(8,128)(2,1)S(1)} %copy-done, f32[1,2560]{1,0:T(1,128)S(1)} %reshape.10.mass_ref, bf16[640,1024]{1,0:T(8,128)(2,1)S(1)} %copy-done.1, bf16[5,128]{1,0:T(8,128)(2,1)S(1)} %bitcast.1, ...), custom_call_target="tpu_custom_call" | custom-call | tf_op jit(solution)/shard_map/pallas_call | solution.py:237
  40.1 0.7 %copy.11 = bf16[64,2560]{1,0:T(8,128)(2,1)} copy(bf16[64,2560]{1,0:T(8,128)(2,1)S(1)} %get-tuple-element.4) | data formatting | bytes 655360
  40.9 0.7 %copy.12 = bf16[640,256]{1,0:T(8,128)(2,1)} copy(bf16[640,256]{1,0:T(8,128)(2,1)S(1)} %get-tuple-element.5) | data formatting | bytes 655360
Async XLA Ops:
  2.0 2.5 %copy-start = (bf16[1024,2560]{1,0:T(8,128)(2,1)S(1)}, bf16[1024,2560]{1,0:T(8,128)(2,1)}, u32[]{:S(2)}) copy-start(bf16[1024,2560]{1,0:T(8,128)(2,1)} %vol_ref.1) | copy-start | bytes 15728644
  4.5 1.3 %copy-start.1 = (bf16[640,1024]{1,0:T(8,128)(2,1)S(1)}, bf16[640,1024]{1,0:T(8,128)(2,1)}, u32[]{:S(2)}) copy-start(bf16[640,1024]{1,0:T(8,128)(2,1)} %press_ref.1) | copy-start | bytes 3932164
  5.8 0.8 %copy-start.2 = (bf16[32,1024]{1,0:T(8,128)(2,1)S(1)}, bf16[32,1024]{1,0:T(8,128)(2,1)}, u32[]{:S(2)}) copy-start(bf16[32,1024]{1,0:T(8,128)(2,1)} %modes_ref.1) | copy-start | bytes 196612
  6.6 0.7 %copy-start.3 = (bf16[640]{0:T(1024)(128)(2,1)S(1)}, bf16[640]{0:T(1024)(128)(2,1)}, u32[]{:S(2)}) copy-start(bf16[640]{0:T(1024)(128)(2,1)} %param.10) | copy-start | bytes 3844

commit v2 on v1

v2 whole, which is shorter than its diff:
```python
import functools

import jax
import jax.numpy as jnp
from jax import lax
from jax.experimental import pallas as pl
from jax.experimental.pallas import tpu as pltpu
from jax.sharding import PartitionSpec as P

MESH = pl.DeviceIdType.MESH
F32 = jnp.float32
BF16 = jnp.bfloat16
LANES = 128


def kernel(
    n, lines, pieces,
    modes_ref, vol_ref, mass_ref, press_ref, area_ref, count_ref,
    ext_ref, wall_ref,
    gbuf, perm, vbuf, pbuf, mass, area, wcol,
    w_send, w_recv, w_keep, wy_send, wy_recv, coef,
    p_send, p_recv, p_keep, py_send, py_recv,
    e_send, ex_recv, e_line, ez_recv, inv_row, inv_col,
    load_sem, g_send_sem, g_recv_sem, w_sem, back_sem, p_sem, py_sem, e_send_sem, ex_sem, ez_sem,
):
    cell, snap = lax.axis_index("cells"), lax.axis_index("snap")
    y, core = snap // 2, snap % 2
    group = n // lines
    z, x = cell // group, cell % group
    near = z // 2
    mate = (cell, y * 2 + 1 - core)
    across = (cell, (1 - y) * 2 + core)
    mode_count, depth = perm.shape
    cols = mode_count // 2
    share = mode_count // 4
    per_share = n // 4
    half = pbuf.shape[1]
    width = vbuf.shape[2]
    slots = 2 * half
    parts = gbuf.shape[1]
    part_rows = gbuf.shape[2]

    def remote(src, dst, send, recv, to):
        return pltpu.make_async_remote_copy(
            src_ref=src, dst_ref=dst, send_sem=send, recv_sem=recv,
            device_id=to, device_id_type=MESH,
        )

    pair = near * 2 + 1 - z % 2
    far = [(1 - near) * 2 + z % 2, (1 - near) * 2 + 1 - z % 2]
    along = [at * group + x for at in [pair] + far]
    beside = [z * group + lax.rem(x + d, group) for d in range(1, group)]

    barrier = pltpu.get_barrier_semaphore()
    greeted = [(to, snap) for to in beside + along] + [mate, across]
    for other in greeted:
        pl.semaphore_signal(barrier, inc=1, device_id=other, device_id_type=MESH)

    loads = [
        pltpu.make_async_copy(
            modes_ref.at[pl.ds(i * part_rows, part_rows)], gbuf.at[cell, i], load_sem.at[i]
        )
        for i in range(parts)
    ]
    loads += [
        pltpu.make_async_copy(area_ref, area, load_sem.at[parts]),
        pltpu.make_async_copy(mass_ref, mass, load_sem.at[parts + 1]),
    ]
    press_copies = [
        pltpu.make_async_copy(
            press_ref.at[pl.ds(h * half, half)], pbuf.at[h], load_sem.at[parts + 2 + h]
        )
        for h in range(2)
    ]
    vol_copies = [
        pltpu.make_async_copy(
            vol_ref.at[:, pl.ds(j * width, width)], vbuf.at[j], load_sem.at[parts + 4 + j]
        )
        for j in range(pieces)
    ]
    for copy in loads + press_copies + vol_copies:
        copy.start()

    pl.semaphore_wait(barrier, len(greeted))

    sent = []
    for d, to in enumerate(beside + along):
        for i in range(parts):
            copy = remote(
                modes_ref.at[pl.ds(i * part_rows, part_rows)], gbuf.at[cell, i],
                g_send_sem.at[0, d, i], g_recv_sem.at[cell, i], (to, snap),
            )
            copy.start()
            sent.append(copy)

    def arrived(origin, i, frm):
        remote(
            gbuf.at[origin, i], gbuf.at[origin, i], g_send_sem.at[0, 0, i], g_recv_sem.at[origin, i],
            (frm, snap),
        ).wait_recv()

    def relay(d):
        origin = along[d]
        for i in range(parts):
            arrived(origin, i, origin)
            for e, to in enumerate(beside):
                copy = remote(
                    gbuf.at[origin, i], gbuf.at[origin, i],
                    g_send_sem.at[1 + d, e, i], g_recv_sem.at[origin, i], (to, snap),
                )
                copy.start()
                sent.append(copy)

    def from_side(lines_at):
        for d in range(1, group):
            for at in lines_at:
                for i in range(parts):
                    arrived(at * group + lax.rem(x + d, group), i, z * group + lax.rem(x + d, group))

    def contract(h, modes_half):
        return lax.dot_general(
            pbuf[h], modes_half, (((1,), (1,)), ((), ())), preferred_element_type=F32
        )

    w_mates, w_acrosses = [], []

    def wall(phase, which):
        modes_half = gbuf[pl.ds(which * (n // 2), n // 2)].reshape(cols, depth).astype(BF16)
        w_send[phase] = contract(1 - core, modes_half).astype(BF16)
        copy = remote(
            w_send.at[phase], w_recv.at[phase], w_sem.at[0, phase], w_sem.at[1, phase], mate
        )
        copy.start()
        w_mates.append(copy)
        w_keep[phase] = contract(core, modes_half)

    def wall_pass(phase):
        w_mates[phase].wait_recv()
        wy_send[phase] = (w_keep[phase] + w_recv[phase].astype(F32)).astype(BF16)
        copy = remote(
            wy_send.at[phase], wy_recv.at[phase], w_sem.at[2, phase], w_sem.at[3, phase], across
        )
        copy.start()
        w_acrosses.append(copy)

    def wall_sum(phase, which):
        w_acrosses[phase].wait_recv()
        coef[core, which] = (
            wy_send[phase].astype(F32) + wy_recv[phase].astype(F32)
        ).astype(BF16)

    for copy in loads:
        copy.wait()
    slot_row = lax.broadcasted_iota(jnp.int32, (1, LANES), 1)
    count = count_ref[0]
    area_lanes = jnp.zeros((1, LANES), F32)
    for i in range(slots // LANES):
        row = area[i : i + 1, :].astype(F32)
        row = jnp.where(slot_row + i * LANES < count, row, 0.0)
        area_lanes = area_lanes + row
        wcol[pl.ds(i * LANES, LANES), :] = jnp.broadcast_to(row, (LANES, LANES)).T

    relay(0)
    for copy in press_copies:
        copy.wait()
    from_side([z, pair])
    wall(0, near)
    relay(1)
    wall_pass(0)
    relay(2)
    from_side(far)

    wall(1, 1 - near)

    order = [
        (1 - y) * 2 + 1 - core, y * 2 + 1 - core, (1 - y) * 2 + core, y * 2 + core,
    ]
    for i, s in enumerate(order):
        perm[pl.ds(i * share, share), :] = (
            gbuf[pl.ds(s * per_share, per_share)].reshape(share, depth).astype(BF16)
        )

    p_copies, py_copies = [], []

    def project(j):
        vol_copies[j].wait()
        part = jnp.dot(perm[...], vbuf[j], preferred_element_type=F32)
        p_send[j] = part[: 2 * share].astype(BF16)
        copy = remote(p_send.at[j], p_recv.at[j], p_sem.at[0, j], p_sem.at[1, j], mate)
        copy.start()
        p_copies.append(copy)
        p_keep[j] = part[2 * share :]

    def pass_on(j):
        p_copies[j].wait_recv()
        both = p_keep[j] + p_recv[j].astype(F32)
        py_send[j] = both[:share].astype(BF16)
        copy = remote(py_send.at[j], py_recv.at[j], py_sem.at[0, j], py_sem.at[1, j], across)
        copy.start()
        py_copies.append(copy)
        p_keep[j, share:, :] = both[share:]

    project(0)
    wall_pass(1)
    for j in range(1, pieces):
        project(j)
        pass_on(j - 1)
    pass_on(pieces - 1)

    wall_sum(0, near)
    wall_sum(1, 1 - near)
    w_back = remote(coef.at[core], coef.at[core], back_sem.at[0], back_sem.at[1], mate)
    w_back.start()
    remote(coef.at[1 - core], coef.at[1 - core], back_sem.at[0], back_sem.at[1], mate).wait_recv()

    rows = mode_count // LANES
    each = cols // LANES
    energy = [jnp.zeros((1, cols), F32) for _ in range(2)]
    for h in range(2):
        for lower in range(0, half, 64):
            weight = wcol[h * half + lower : h * half + lower + 64, 0:1]
            for m in range(2):
                value = coef[h, m, lower : lower + 64, :].astype(F32)
                energy[m] = energy[m] + jnp.sum(weight * value * value, axis=0, keepdims=True)
    e_send[...] = jnp.concatenate(
        [energy[i // each][:, (i % each) * LANES : (i % each + 1) * LANES] for i in range(rows)]
        + [area_lanes, jnp.zeros((8 - rows - 1, LANES), F32)],
        axis=0,
    )
    e_copies = []

    def gather_sum(src, slots_ref, at, sems, base, peers):
        slots_ref[at] = src[...]
        for d, (to, _) in enumerate(peers):
            copy = remote(src, slots_ref.at[at], e_send_sem.at[base + d], sems.at[at], (to, snap))
            copy.start()
            e_copies.append(copy)
        for to, slot in peers:
            remote(
                src, slots_ref.at[slot], e_send_sem.at[base], sems.at[slot], (to, snap)
            ).wait_recv()
        return jnp.sum(slots_ref[...], axis=0)

    e_line[...] = gather_sum(
        e_send, ex_recv, x, ex_sem, 0,
        [(to, lax.rem(x + 1 + d, group)) for d, to in enumerate(beside)],
    )
    total = gather_sum(
        e_line, ez_recv, z, ez_sem, group - 1, list(zip(along, [pair] + far))
    )
    area_total = jnp.sum(total[rows : rows + 1, :], axis=1, keepdims=True)
    inverse = lax.rsqrt(total[:rows, :] / area_total + 1e-06)
    inv_row[...] = inverse.reshape(rows, 1, LANES)

    for m in range(2):
        flat = jnp.concatenate([inverse[i : i + 1, :] for i in range(m * each, (m + 1) * each)], axis=1)
        for h in range(2):
            for lower in range(0, half, 64):
                at = h * half + lower
                live = lax.broadcasted_iota(jnp.int32, (64, 1), 0) + at < count
                value = coef[h, m, lower : lower + 64, :].astype(F32) * flat
                wall_ref[at : at + 64, m * cols : (m + 1) * cols] = jnp.where(
                    live, value, 0.0
                ).astype(BF16)

    turned = jnp.broadcast_to(inv_row[y], (LANES, LANES)).T
    inv_col[...] = turned.reshape(2, share, LANES)
    mine = inv_col[core]
    for j in range(pieces):
        py_copies[j].wait_recv()
        for i in range(width // LANES):
            at = slice(i * LANES, (i + 1) * LANES)
            row = j * (width // LANES) + i
            summed = p_keep[j, share:, at] + py_recv[j, :, at].astype(F32)
            scaled = summed * mass[row : row + 1, :] * mine
            ext_ref[:, row * LANES : (row + 1) * LANES] = scaled.astype(BF16)

    for copy in sent + w_mates + w_acrosses + [w_back] + p_copies + py_copies + e_copies:
        copy.wait_send()


def deliver(ext_in, wall_in, ext_out, wall_out, sems):
    copies = [
        pltpu.make_async_copy(ext_in, ext_out, sems.at[0]),
        pltpu.make_async_copy(wall_in, wall_out, sems.at[1]),
    ]
    for copy in copies:
        copy.start()
    for copy in copies:
        copy.wait()


def body(n, temporal_modes, volume_field, mass_root, wall_pressure, face_area, face_count):
    rows, depth = temporal_modes.shape
    mode_count = rows * n
    cells = volume_field.shape[1]
    slots = wall_pressure.shape[0]
    half = slots // 2
    lines = 4
    pieces = 5
    width = cells // pieces
    share = mode_count // 4
    cols = mode_count // 2
    moved = BF16 if rows % 16 == 0 else F32
    parts = 2 if rows % 32 == 0 else 1
    group = n // lines
    dma = pltpu.SemaphoreType.DMA
    hbm, vmem, smem, anywhere = (
        pl.BlockSpec(memory_space=m) for m in (pltpu.HBM, pltpu.VMEM, pltpu.SMEM, pl.ANY)
    )
    shapes = (
        jax.ShapeDtypeStruct((share, cells), BF16),
        jax.ShapeDtypeStruct((slots, mode_count), BF16),
    )
    results = pl.pallas_call(
        functools.partial(kernel, n, lines, pieces),
        out_shape=tuple(pltpu.VMEM(s.shape, s.dtype) for s in shapes),
        in_specs=[hbm] * 5 + [smem],
        out_specs=(vmem, vmem),
        scratch_shapes=[
            pltpu.VMEM((n, parts, rows // parts, depth), moved),
            pltpu.VMEM((mode_count, depth), BF16),
            pltpu.VMEM((pieces, depth, width), BF16),
            pltpu.VMEM((2, half, depth), BF16),
            pltpu.VMEM((cells // LANES, LANES), F32),
            pltpu.VMEM((slots // LANES, LANES), BF16),
            pltpu.VMEM((slots, LANES), F32),
            pltpu.VMEM((2, half, cols), BF16),
            pltpu.VMEM((2, half, cols), BF16),
            pltpu.VMEM((2, half, cols), F32),
            pltpu.VMEM((2, half, cols), BF16),
            pltpu.VMEM((2, half, cols), BF16),
            pltpu.VMEM((2, 2, half, cols), BF16),
            pltpu.VMEM((pieces, 2 * share, width), BF16),
            pltpu.VMEM((pieces, 2 * share, width), BF16),
            pltpu.VMEM((pieces, 2 * share, width), F32),
            pltpu.VMEM((pieces, share, width), BF16),
            pltpu.VMEM((pieces, share, width), BF16),
            pltpu.VMEM((8, LANES), F32),
            pltpu.VMEM((group, 8, LANES), F32),
            pltpu.VMEM((8, LANES), F32),
            pltpu.VMEM((lines, 8, LANES), F32),
            pltpu.VMEM((mode_count // LANES, 1, LANES), F32),
            pltpu.VMEM((2, share, LANES), F32),
            dma((parts + 4 + pieces,)),
            dma((lines, group - 1 + lines - 1, parts)),
            dma((n, parts)),
            dma((4, 2)),
            dma((2,)),
            dma((2, pieces)),
            dma((2, pieces)),
            dma((group - 1 + lines - 1,)),
            dma((group,)),
            dma((lines,)),
        ],
        compiler_params=pltpu.CompilerParams(
            collective_id=0, has_side_effects=True, vmem_limit_bytes=58 * 1024 * 1024
        ),
    )(
        temporal_modes.astype(moved),
        volume_field,
        mass_root.reshape(cells // LANES, LANES),
        wall_pressure,
        face_area.reshape(slots // LANES, LANES),
        face_count,
    )
    return pl.pallas_call(
        deliver,
        out_shape=shapes,
        in_specs=[vmem, vmem],
        out_specs=(anywhere, anywhere),
        scratch_shapes=[dma((2,))],
        compiler_params=pltpu.CompilerParams(vmem_limit_bytes=1024 * 1024),
    )(*results)


def solution(mesh):
    in_specs = (
        P("cells", "snap"),
        P("snap", "cells"),
        P("cells"),
        P("cells", "snap"),
        P("cells"),
        P("cells"),
    )
    out_specs = (P("snap", "cells"), P("cells", None))
    return jax.shard_map(
        functools.partial(body, mesh.shape["cells"]),
        mesh=mesh, in_specs=in_specs, out_specs=out_specs, check_vma=False,
    )
```

time: 41.9 us -> 34.4 us (0.82)
  local copies, waits for them, and re-layouts: 7.48 us -> 0 us
    unnamed x10 -> x0, local copies, waits for them, and re-layouts: 6.77 us -> none
    reshape x1 -> x0, local copies, waits for them, and re-layouts: 0.72 us -> none  [body(): mass_root.reshape(1, cells)]
    pallas_call x1 -> x2, Pallas kernels: 32.8 us -> 32.9 us  [the longest x1 32.1 us: body(): pl.pallas_call(functools.partial(kernel, n, lines, pieces), out_shape=tup...]
where the time goes in v2:
time: 34.4 us; the launch traced here: 34.2 us
  Pallas kernels  32.9 us (96%)
  between operations  1.29 us (4%)
    pallas_call x1, Pallas kernels, body(): pl.pallas_call(functools.partial(kernel, n, lines, pieces), out_shape=tup...  32.1 us
    pallas_call x1, Pallas kernels, body(): pl.pallas_call(deliver, out_shape=shapes, in_specs=[vmem, vmem], out_spec...  0.85 us

profile of v2, /device:TPU:0, one launch (start us, length us, event | category | flops | bytes accessed | tf_op | source)
XLA Modules:
  0.0 34.2 jit_solution(14406853782326189525)
XLA Ops:
  1.3 32.1 %shard_map.77 = (bf16[64,2560]{1,0:T(8,128)(2,1)S(1)}, bf16[640,256]{1,0:T(8,128)(2,1)S(1)}) custom-call(bf16[32,1024]{1,0:T(8,128)(2,1)} %modes_ref.1, bf16[1024,2560]{1,0:T(8,128)(2,1)} %vol_ref.1, f32[20,128]{1,0:T(8,128)} %bitcast.2, bf16[640,1024]{1,0:T(8,128)(2,1)} %press_ref.1, bf16[5,128]{1,0:T(8,128)(2,1)} %bitcast.3, s32[1]{0:T(128)S(6)} %copy.8.count_ref), custom_call_target="tpu_custom_call" | custom-call | tf_op jit(solution)/shard_map/pallas_call | solution.py:315
  33.3 0.9 %shard_map.78 = (bf16[64,2560]{1,0:T(8,128)(2,1)}, bf16[640,256]{1,0:T(8,128)(2,1)}) custom-call(bf16[64,2560]{1,0:T(8,128)(2,1)S(1)} %get-tuple-element.4.ext_in, bf16[640,256]{1,0:T(8,128)(2,1)S(1)} %get-tuple-element.5.wall_in), custom_call_target="tpu_custom_call" | custom-call | tf_op jit(solution)/shard_map/pallas_call | solution.py:367

commit v3 on v2

--- a/solution.py
+++ b/solution.py
@@ -84,7 +84,7 @@
     pl.semaphore_wait(barrier, len(greeted))
 
     sent = []
-    for d, to in enumerate(beside + along):
+    for d, to in enumerate(beside + along[1:] + along[:1]):
         for i in range(parts):
             copy = remote(
                 modes_ref.at[pl.ds(i * part_rows, part_rows)], gbuf.at[cell, i],
@@ -160,14 +160,14 @@
         area_lanes = area_lanes + row
         wcol[pl.ds(i * LANES, LANES), :] = jnp.broadcast_to(row, (LANES, LANES)).T
 
+    relay(1)
     relay(0)
+    relay(2)
     for copy in press_copies:
         copy.wait()
     from_side([z, pair])
     wall(0, near)
-    relay(1)
     wall_pass(0)
-    relay(2)
     from_side(far)
 
     wall(1, 1 - near)
@@ -297,7 +297,7 @@
     slots = wall_pressure.shape[0]
     half = slots // 2
     lines = 4
-    pieces = 5
+    pieces = 4
     width = cells // pieces
     share = mode_count // 4
     cols = mode_count // 2

time: 34.4 us -> 33.4 us (0.971)
  Pallas kernels: 32.9 us -> 31.9 us
    pallas_call x1, Pallas kernels: 32.1 us -> 31.1 us  [body(): pl.pallas_call(functools.partial(kernel, n, lines, pieces), out_shape=tup...]
where the time goes in v3:
time: 33.4 us; the launch traced here: 33.2 us
  Pallas kernels  31.9 us (96%)
  between operations  1.29 us (4%)
    pallas_call x1, Pallas kernels, body(): pl.pallas_call(functools.partial(kernel, n, lines, pieces), out_shape=tup...  31.1 us
    pallas_call x1, Pallas kernels, body(): pl.pallas_call(deliver, out_shape=shapes, in_specs=[vmem, vmem], out_spec...  0.85 us

profile of v3, /device:TPU:0, one launch (start us, length us, event | category | flops | bytes accessed | tf_op | source)
XLA Modules:
  0.0 33.2 jit_solution(18346951846156053324)
XLA Ops:
  1.3 31.1 %shard_map.77 = (bf16[64,2560]{1,0:T(8,128)(2,1)S(1)}, bf16[640,256]{1,0:T(8,128)(2,1)S(1)}) custom-call(bf16[32,1024]{1,0:T(8,128)(2,1)} %modes_ref.1, bf16[1024,2560]{1,0:T(8,128)(2,1)} %vol_ref.1, f32[20,128]{1,0:T(8,128)} %bitcast.2, bf16[640,1024]{1,0:T(8,128)(2,1)} %press_ref.1, bf16[5,128]{1,0:T(8,128)(2,1)} %bitcast.3, s32[1]{0:T(128)S(6)} %copy.8.count_ref), custom_call_target="tpu_custom_call" | custom-call | tf_op jit(solution)/shard_map/pallas_call | solution.py:315
  32.4 0.9 %shard_map.78 = (bf16[64,2560]{1,0:T(8,128)(2,1)}, bf16[640,256]{1,0:T(8,128)(2,1)}) custom-call(bf16[64,2560]{1,0:T(8,128)(2,1)S(1)} %get-tuple-element.4.ext_in, bf16[640,256]{1,0:T(8,128)(2,1)S(1)} %get-tuple-element.5.wall_in), custom_call_target="tpu_custom_call" | custom-call | tf_op jit(solution)/shard_map/pallas_call | solution.py:367

commit v4 on v3

--- a/solution.py
+++ b/solution.py
@@ -200,17 +200,22 @@
         py_copies.append(copy)
         p_keep[j, share:, :] = both[share:]
 
+    def wall_back():
+        wall_sum(0, near)
+        wall_sum(1, 1 - near)
+        copy = remote(coef.at[core], coef.at[core], back_sem.at[0], back_sem.at[1], mate)
+        copy.start()
+        return copy
+
     project(0)
     wall_pass(1)
     for j in range(1, pieces):
         project(j)
         pass_on(j - 1)
+    w_back = wall_back()
     pass_on(pieces - 1)
 
-    wall_sum(0, near)
-    wall_sum(1, 1 - near)
-    w_back = remote(coef.at[core], coef.at[core], back_sem.at[0], back_sem.at[1], mate)
-    w_back.start()
+
     remote(coef.at[1 - core], coef.at[1 - core], back_sem.at[0], back_sem.at[1], mate).wait_recv()
 
     rows = mode_count // LANES

time: 33.4 us -> 33.4 us (level)
  no operation moved by 1% of the time
where the time goes in v4:
time: 33.4 us; the launch traced here: 33.2 us
  Pallas kernels  31.9 us (96%)
  between operations  1.29 us (4%)
    pallas_call x1, Pallas kernels, body(): pl.pallas_call(functools.partial(kernel, n, lines, pieces), out_shape=tup...  31.1 us
    pallas_call x1, Pallas kernels, body(): pl.pallas_call(deliver, out_shape=shapes, in_specs=[vmem, vmem], out_spec...  0.85 us

profile of v4, /device:TPU:0, one launch (start us, length us, event | category | flops | bytes accessed | tf_op | source)
XLA Modules:
  0.0 33.2 jit_solution(13165772379108043348)
XLA Ops:
  1.3 31.1 %shard_map.77 = (bf16[64,2560]{1,0:T(8,128)(2,1)S(1)}, bf16[640,256]{1,0:T(8,128)(2,1)S(1)}) custom-call(bf16[32,1024]{1,0:T(8,128)(2,1)} %modes_ref.1, bf16[1024,2560]{1,0:T(8,128)(2,1)} %vol_ref.1, f32[20,128]{1,0:T(8,128)} %bitcast.2, bf16[640,1024]{1,0:T(8,128)(2,1)} %press_ref.1, bf16[5,128]{1,0:T(8,128)(2,1)} %bitcast.3, s32[1]{0:T(128)S(6)} %copy.8.count_ref), custom_call_target="tpu_custom_call" | custom-call | tf_op jit(solution)/shard_map/pallas_call | solution.py:320
  32.4 0.9 %shard_map.78 = (bf16[64,2560]{1,0:T(8,128)(2,1)}, bf16[640,256]{1,0:T(8,128)(2,1)}) custom-call(bf16[64,2560]{1,0:T(8,128)(2,1)S(1)} %get-tuple-element.4.ext_in, bf16[640,256]{1,0:T(8,128)(2,1)S(1)} %get-tuple-element.5.wall_in), custom_call_target="tpu_custom_call" | custom-call | tf_op jit(solution)/shard_map/pallas_call | solution.py:372
